TPU v7x, 128 devices: a whole 4x4x4 slice. The times are simulated.
128 devices in a mesh: lat: 4 (over z), lon: 32 (over x, y, core).
Axes of the slice: x: 4, y: 4, z: 4, core: 2. Of those that a mesh axis runs over, the one named last changes fastest.
Arguments:
- obs_tiles: bfloat16 [128, 128, 4, 8, 256], P(('lat', 'lon'))
- tile_block: int32 [128, 128, 4], P(('lat', 'lon')), may hold values from 0 to 11
- tile_rows: int32 [128, 128, 4], P(('lat', 'lon')), may hold values from 0 to 256, as said below
- embed_weight: bfloat16 [6, 23], replicated, may hold values from -2.5 to 2.5
- conv1_weight: bfloat16 [9, 24, 256], replicated, may hold values from -0.4375 to 0.4375
- conv1_bias: float32 [256], replicated, may hold values from -3 to 3
- conv2_weight: bfloat16 [9, 256, 512], replicated, may hold values from -0.125 to 0.125
- conv2_bias: float32 [512], replicated, may hold values from -3 to 3
Outputs:
- coarse: bfloat16 [64, 384, 512], P('lat')
Inputs may be any that keep to these rules, and one draw needn't show every extreme that they name: `tile_rows`: for each source and destination the live slots come first: all hold 256 rows but the last live one, which holds 1 to 256; later slots hold 0. In every draw one destination block receives 4 live tiles from every source.
All inputs are finite; a program needn't handle non-finite values.
Results may differ from a plain program's by a relative error of at most 0.0052.
Values may be sent and summed in bfloat16 or wider, within the bound.
No kernel may reach another device: no remote copies, remote signals or barrier semaphores. Data moves between devices by JAX's collectives and lax.ppermute only.
A program may use at most 64 MiB of HBM per device.

v0:
```python
import jax
import jax.numpy as jnp
from jax import lax
from jax.sharding import PartitionSpec as P

BX = 64
BY = 48
SB = 16
kernel_scale = 0.5


def shifted(value, axis, by):
    length = lax.axis_size(axis)
    return lax.ppermute(value, axis, [(i, (i + by) % length) for i in range(length)])


def from_behind(block, axis, distance):
    devices = range(lax.axis_size(axis))
    route = [(i - distance, i) for i in devices if i - distance in devices]
    return lax.ppermute(block, axis, route)


def tile_terms(tiles, row_count, embed_weight):
    cell_ids = jnp.arange(SB * SB, dtype=jnp.int32)
    center_row = (cell_ids // SB).astype(jnp.float32) + 0.5
    center_col = (cell_ids % SB).astype(jnp.float32) + 0.5
    place_row = tiles[:, 0, :].astype(jnp.float32)
    place_col = tiles[:, 1, :].astype(jnp.float32)
    distance = (center_row[None, :, None] - place_row[:, None, :]) ** 2 + (
        center_col[None, :, None] - place_col[:, None, :]
    ) ** 2
    is_live = jnp.arange(tiles.shape[2], dtype=jnp.int32)[None, None, :] < row_count[:, None, None]
    kernel = jnp.where(is_live, jnp.exp(-distance * kernel_scale), jnp.float32(0.0)).astype(
        jnp.bfloat16
    )
    embedded = jnp.einsum(
        "tvo,vc->tco", tiles[:, 2:, :], embed_weight, preferred_element_type=jnp.float32
    ).astype(jnp.bfloat16)
    features = jnp.concatenate(
        [jnp.ones((tiles.shape[0], 1, tiles.shape[2]), jnp.bfloat16), embedded], axis=1
    )
    return jnp.einsum("tco,tko->tck", features, kernel, preferred_element_type=jnp.float32)


def stride_conv(padded, weight, out_rows, out_cols):
    running = jnp.zeros((out_rows * out_cols, weight.shape[2]), jnp.float32)
    for row_tap in range(3):
        for col_tap in range(3):
            tap_rows = lax.slice(
                padded,
                (row_tap, col_tap, 0),
                (row_tap + 2 * out_rows - 1, col_tap + 2 * out_cols - 1, padded.shape[2]),
                (2, 2, 1),
            )
            running = running + jnp.dot(
                tap_rows.reshape(-1, padded.shape[2]),
                weight[3 * row_tap + col_tap],
                preferred_element_type=jnp.float32,
            )
    return running.reshape(out_rows, out_cols, weight.shape[2])


def shards(
    obs_tiles,
    tile_block,
    tile_rows,
    embed_weight,
    conv1_weight,
    conv1_bias,
    conv2_weight,
    conv2_bias,
):
    block_count = obs_tiles.shape[1]
    slot_count = obs_tiles.shape[2]
    feat_rows = obs_tiles.shape[3]
    tile_len = obs_tiles.shape[4]
    arrived_all = (
        lax.all_to_all(obs_tiles, ("lat", "lon"), split_axis=1, concat_axis=0, tiled=True),
        lax.all_to_all(tile_block, ("lat", "lon"), split_axis=1, concat_axis=0, tiled=True),
        lax.all_to_all(tile_rows, ("lat", "lon"), split_axis=1, concat_axis=0, tiled=True),
    )
    group_count = block_count // 8
    group_size = 8 * slot_count
    arrived = arrived_all[0].reshape(group_count, group_size, feat_rows, tile_len)
    block_ids = arrived_all[1].reshape(group_count, group_size)
    row_count = arrived_all[2].reshape(group_count, group_size)
    sub_count = BX // SB * (BY // SB)
    channel_count = conv1_weight.shape[1]

    def add_group(running, inputs):
        tiles, group_ids, group_rows = inputs
        tile_sums = tile_terms(tiles, group_rows, embed_weight)
        onehot = (group_ids[:, None] == jnp.arange(sub_count, dtype=jnp.int32)[None, :]).astype(
            jnp.float32
        )
        return (
            running + jnp.einsum("ts,tck->sck", onehot, tile_sums, precision=lax.Precision.HIGHEST),
            None,
        )

    start = jnp.zeros((sub_count, channel_count, tile_len), jnp.float32)
    block_sums, _ = lax.scan(add_group, start, (arrived, block_ids, row_count))
    density = block_sums[:, 0, :]
    data_part = block_sums[:, 1:, :] / (1.0 + density[:, None, :])
    channels = jnp.concatenate([jnp.log1p(density)[:, None, :], data_part], axis=1).astype(
        jnp.bfloat16
    )
    grid_field = (
        channels.reshape(BX // SB, BY // SB, channel_count, SB, SB)
        .transpose(0, 3, 1, 4, 2)
        .reshape(BX, BY, channel_count)
    )
    rim_width = 1
    side_rim = shifted(grid_field[:, BY - rim_width :, :], "lon", 1)
    padded = jnp.concatenate([side_rim, grid_field], axis=1)
    top_rim = from_behind(padded[BX - rim_width :, :, :], "lat", 1)
    padded = jnp.concatenate([top_rim, padded], axis=0)
    first_layer = jax.nn.silu(
        stride_conv(padded, conv1_weight, BX // 2, BY // 2) + conv1_bias
    ).astype(jnp.bfloat16)
    first_side = shifted(first_layer[:, BY // 2 - 1 :, :], "lon", 1)
    first_padded = jnp.concatenate([first_side, first_layer], axis=1)
    first_top = from_behind(first_padded[BX // 2 - 1 :, :, :], "lat", 1)
    first_padded = jnp.concatenate([first_top, first_padded], axis=0)
    coarse = (stride_conv(first_padded, conv2_weight, BX // 4, BY // 4) + conv2_bias).astype(
        jnp.bfloat16
    )
    return lax.all_gather(coarse, "lon", axis=1, tiled=True)


def solution(mesh):
    placed = (
        P(("lat", "lon"), None, None, None, None),
        P(("lat", "lon"), None, None),
        P(("lat", "lon"), None, None),
        P(),
        P(),
        P(),
        P(),
        P(),
    )
    return jax.shard_map(
        shards, mesh=mesh, in_specs=placed, out_specs=P("lat", None, None), check_vma=False
    )
```

profile of v0, /device:TPU:1, one launch (start us, length us, event | category | flops | bytes accessed | tf_op | source)
XLA Modules:
  0.0 268.7 jit_solution(6266015869091623327)
XLA Ops:
  8.0 11.5 %all-to-all-start = ((s32[1,128,4]{2,0,1:T(1,128)}), s32[1,128,4]{2,0,1:T(1,128)S(1)}, u32[]{:S(2)}, u32[]{:S(2)}) async-start(s32[1,128,4]{2,0,1:T(1,128)} %copy.26), calls=%async_computation | async-start | bytes 131072 | tf_op jit(solution)/shard_map/all_to_all | solution.py:79
  20.3 8.7 %all-to-all-done = s32[1,128,4]{2,0,1:T(1,128)S(1)} async-done(((s32[1,128,4]{2,0,1:T(1,128)}), s32[1,128,4]{2,0,1:T(1,128)S(1)}, u32[]{:S(2)}, u32[]{:S(2)}) %all-to-all-start) | async-done | bytes 2080 | tf_op jit(solution)/shard_map/all_to_all | solution.py:79
  29.0 13.8 %all_to_all.12 = s32[1,128,4]{2,0,1:T(1,128)S(1)} all-to-all(s32[1,128,4]{2,0,1:T(1,128)S(1)} %copy.28), channel_id=1, replica_groups=mesh['lat'=4,'lon'=32] {'lat','lon'}, dimensions={1} | all-to-all | bytes 4096 | tf_op jit(solution)/shard_map/all_to_all | solution.py:80
  42.8 4.4 %all-to-all-start.1 = ((bf16[1,128,4,8,256]{4,3,2,0,1:T(8,128)(2,1)}), bf16[1,128,4,8,256]{4,3,2,0,1:T(8,128)(2,1)S(1)}, u32[]{:S(2)}, u32[]{:S(2)}) async-start(bf16[1,128,4,8,256]{4,3,2,0,1:T(8,128)(2,1)} %bitcast.136), calls=%async_computation.1 | async-start | bytes 4194304 | tf_op jit(solution)/shard_map/all_to_all | solution.py:78
  49.5 28.2 %all-to-all-done.1 = bf16[1,128,4,8,256]{4,3,2,0,1:T(8,128)(2,1)S(1)} async-done(((bf16[1,128,4,8,256]{4,3,2,0,1:T(8,128)(2,1)}), bf16[1,128,4,8,256]{4,3,2,0,1:T(8,128)(2,1)S(1)}, u32[]{:S(2)}, u32[]{:S(2)}) %all-to-all-start.1) | async-done | bytes 2097184 | tf_op jit(solution)/shard_map/all_to_all | solution.py:78
  77.7 61.0 %while.13 = (s32[]{:T(128)}, f32[12,24,256]{2,0,1:T(8,128)S(1)}, s32[16,32]{1,0:T(8,128)S(1)}, bf16[16,32,8,256]{3,2,1,0:T(8,128)(2,1)S(1)}, bf16[6,23]{1,0:T(8,...) while((s32[]{:T(128)}, f32[12,24,256]{2,0,1:T(8,128)S(1)}, ...), condition=%wide.region_1.2_spmd.clone, body=%wide.region_0.1_spmd.clone.sunk | while | flops 150475136 | bytes 3626115 | solution.py:102
  78.2 2.7 fusion.104
  82.0 2.7 fusion.104
  89.6 2.7 fusion.104
  93.5 2.7 fusion.104
  97.3 2.7 fusion.104
  101.1 2.7 fusion.104
  104.9 2.7 fusion.104
  108.7 2.7 fusion.104
  112.5 2.7 fusion.104
  116.3 2.7 fusion.104
  120.2 2.7 fusion.104
  156.7 3.7 %slice.160 = bf16[32,24,24]{0,2,1:T(8,128)(2,1)S(1)} slice(bf16[64,49,24]{0,2,1:T(8,128)(2,1)S(1)} %pad_maximum_fusion.1), slice={[1:64:2], [0:47:2], [0:24:1]} | slice | bytes 73728 | tf_op jit(solution)/shard_map/slice | solution.py:49
  160.4 3.7 %slice.154 = bf16[32,24,24]{0,2,1:T(8,128)(2,1)S(1)} slice(bf16[64,49,24]{0,2,1:T(8,128)(2,1)S(1)} %pad_maximum_fusion.1), slice={[0:63:2], [0:47:2], [0:24:1]} | slice | bytes 73728 | tf_op jit(solution)/shard_map/slice | solution.py:49
  167.3 4.2 %slice.152 = bf16[32,24,24]{0,2,1:T(8,128)(2,1)S(1)} slice(bf16[65,49,24]{0,2,1:T(8,128)(2,1)S(1)} %maximum_maximum_fusion.1), slice={[0:63:2], [2:49:2], [0:24:1]} | slice | bytes 73728 | tf_op jit(solution)/shard_map/slice | solution.py:49
  171.5 3.7 %slice.150 = bf16[32,24,24]{0,2,1:T(8,128)(2,1)S(1)} slice(bf16[65,49,24]{0,2,1:T(8,128)(2,1)S(1)} %maximum_maximum_fusion.1), slice={[0:63:2], [1:48:2], [0:24:1]} | slice | bytes 73728 | tf_op jit(solution)/shard_map/slice | solution.py:49
  175.2 3.7 %slice.148 = bf16[32,24,24]{0,2,1:T(8,128)(2,1)S(1)} slice(bf16[65,49,24]{0,2,1:T(8,128)(2,1)S(1)} %maximum_maximum_fusion.1), slice={[0:63:2], [0:47:2], [0:24:1]} | slice | bytes 73728 | tf_op jit(solution)/shard_map/slice | solution.py:49
  201.4 51.4 %all-gather.2.cloned.1.call-done = bf16[16,384,512]{2,0,1:T(8,128)(2,1)} async-done(((bf16[16,12,512]{2,0,1:T(8,128)(2,1)}), bf16[16,384,512]{2,0,1:T(8,128)(2,1)}) %all-gather.2.cloned.1.call-update) | async-done | bytes 6291472 | tf_op jit(solution)/shard_map/all_gather | solution.py:128
  252.8 9.0 %copy.39 = bf16[16,384,512]{2,1,0:T(8,128)(2,1)} copy(bf16[16,384,512]{2,0,1:T(8,128)(2,1)} %all-gather.2.cloned.1.call-done) | data formatting | bytes 12582912 | tf_op jit(solution)/shard_map/all_gather | solution.py:128
  (248 shorter events, 78.4 us)
Async XLA Ops:
  8.0 21.0 %all-to-all-start = ((s32[1,128,4]{2,0,1:T(1,128)}), s32[1,128,4]{2,0,1:T(1,128)S(1)}, u32[]{:S(2)}, u32[]{:S(2)}) async-start(s32[1,128,4]{2,0,1:T(1,128)} %copy.26), calls=%async_computation | async-start | bytes 131072 | tf_op jit(solution)/shard_map/all_to_all | solution.py:79
  20.2 57.5 %copy-start.10 = (bf16[6,23]{1,0:T(8,128)(2,1)S(1)}, bf16[6,23]{1,0:T(8,128)(2,1)}, u32[]{:S(2)}) copy-start(bf16[6,23]{1,0:T(8,128)(2,1)} %param.13) | copy-start | bytes 832
  42.8 34.9 %all-to-all-start.1 = ((bf16[1,128,4,8,256]{4,3,2,0,1:T(8,128)(2,1)}), bf16[1,128,4,8,256]{4,3,2,0,1:T(8,128)(2,1)S(1)}, u32[]{:S(2)}, u32[]{:S(2)}) async-start(bf16[1,128,4,8,256]{4,3,2,0,1:T(8,128)(2,1)} %bitcast.136), calls=%async_computation.1 | async-start | bytes 4194304 | tf_op jit(solution)/shard_map/all_to_all | solution.py:78
  47.2 205.6 %all-gather.2.cloned.1.call-start = ((), (), s32[]{:S(2)}) async-start(), calls=%async_computation.3 | async-start | bytes 6488064 | tf_op jit(solution)/shard_map/all_gather | solution.py:128
  146.8 6.2 %collective-permute-start = (bf16[64,1,24]{2,1,0:T(2,128)(2,1)}, bf16[64,1,24]{2,1,0:T(2,128)(2,1)}, u32[]{:S(2)}, u32[]{:S(2)}) collective-permute-start(bf16[64,1,24]{2,1,0:T(2,128)(2,1)} %slice.192), channel_id=1, source_target_pairs={{0,1},{1,2},{2,3},{3,4},{4,5},{5,6},{6,7},{7,8},{8,9},{9,10},{10,1... | collective-permute-start | bytes 9224 | tf_op jit(solution)/shard_map/ppermute | solution.py:14
  154.7 11.5 %collective-permute-start.1 = (bf16[1,49,24]{0,2,1:T(8,128)(2,1)}, bf16[1,49,24]{0,2,1:T(8,128)(2,1)}, u32[]{:S(2)}, u32[]{:S(2)}) collective-permute-start(bf16[1,49,24]{0,2,1:T(8,128)(2,1)} %fusion.25), channel_id=1, source_target_pairs={{0,32},{32,64},{64,96},{1,33},{33,65},{65,97},{2,34},{34,66},{66,9... | collective-permute-start | bytes 7064 | tf_op jit(solution)/shard_map/ppermute | solution.py:20
  180.3 3.5 %copy-start = (f32[768,256]{1,0:T(8,128)S(1)}, f32[768,256]{1,0:T(8,128)}, u32[]{:S(2)}) copy-start(f32[768,256]{1,0:T(8,128)} %fusion.51) | copy-start | bytes 2359300
  180.5 3.4 %copy-start.9 = (bf16[768,24]{0,1:T(8,128)(2,1)S(1)}, bf16[768,24]{0,1:T(8,128)(2,1)}, u32[]{:S(2)}) copy-start(bf16[768,24]{0,1:T(8,128)(2,1)} %reshape.154) | copy-start | bytes 110596
  182.8 2.1 copy-start.8
  184.9 1.0 copy-start.12
  186.2 5.1 %collective-permute-start.2 = (bf16[32,1,256]{2,1,0:T(2,128)(2,1)S(1)}, bf16[32,1,256]{2,1,0:T(2,128)(2,1)S(1)}, u32[]{:S(2)}, u32[]{:S(2)}) collective-permute-start(bf16[32,1,256]{2,1,0:T(2,128)(2,1)S(1)} %slice.195), channel_id=1, source_target_pairs={{0,1},{1,2},{2,3},{3,4},{4,5},{5,6},{6,7},{7,8},{8,9},{9,10},{10,1... | collective-permute-start | bytes 49160 | tf_op jit(solution)/shard_map/ppermute | solution.py:14
  191.3 7.1 %copy-start.1 = (bf16[9,256,512]{2,1,0:T(8,128)(2,1)S(1)}, bf16[9,256,512]{2,1,0:T(8,128)(2,1)}, u32[]{:S(2)}) copy-start(bf16[9,256,512]{2,1,0:T(8,128)(2,1)} %param.16) | copy-start | bytes 7077892
  191.3 2.7 copy-start.7
  191.9 4.1 %collective-permute-start.3 = (bf16[1,25,256]{2,1,0:T(8,128)(2,1)}, bf16[1,25,256]{2,1,0:T(8,128)(2,1)S(1)}, u32[]{:S(2)}, u32[]{:S(2)}) collective-permute-start(bf16[1,25,256]{2,1,0:T(8,128)(2,1)} %fusion.45), channel_id=1, source_target_pairs={{0,32},{32,64},{64,96},{1,33},{33,65},{65,97},{2,34},{34,66},{66,9... | collective-permute-start | bytes 38408 | tf_op jit(solution)/shard_map/ppermute | solution.py:20
  197.0 2.0 copy-start.6
  198.3 1.0 copy-start.5
  198.6 0.9 copy-start.4
  199.1 0.9 copy-start.3
  199.3 0.9 copy-start.2
  199.7 0.7 copy-start.11
Sparse Core Ops, SparseCore 0:
  201.5 51.2 all-gather.1
where the time goes:
time: 270 us; the launch traced here: 269 us
  waiting for transfers between devices  88.4 us (33%)
  matrix products  69.2 us (26%)
  local copies, waits for them, and re-layouts  53.3 us (20%)
  starting transfers between devices  20.9 us (8%)
  between operations  14 us (5%)
  blocking collectives  13.8 us (5%)
  other arithmetic  7.95 us (3%)
    all_gather x1, waiting for transfers between devices, shards(): return lax.all_gather(coarse, 'lon', axis=1, tiled=True)  51.4 us
    dot_general x16, matrix products, tile_terms(): jnp.einsum('tco,tko->tck', features, kernel, preferred_element_type=jnp.f...  42.6 us
    slice x23, local copies, waits for them, and re-layouts, stride_conv(): lax.slice(padded, (row_tap, col_tap, 0), (row_tap + 2 * out_rows - 1, col...  29.3 us
    all_to_all x1, waiting for transfers between devices, shards(): lax.all_to_all(obs_tiles, ('lat', 'lon'), split_axis=1, concat_axis=0, ti...  28.2 us
    all_to_all x1, blocking collectives, shards(): lax.all_to_all(tile_rows, ('lat', 'lon'), split_axis=1, concat_axis=0, ti...  13.8 us
    dot_general x18, matrix products, stride_conv(): jnp.dot(tap_rows.reshape(-1, padded.shape[2]), weight[3 * row_tap + col_t...  11.6 us
    all_to_all x1, starting transfers between devices, shards(): lax.all_to_all(tile_block, ('lat', 'lon'), split_axis=1, concat_axis=0, t...  11.5 us
    dot_general x16, matrix products, add_group(): jnp.einsum('ts,tck->sck', onehot, tile_sums, precision=lax.Precision.HIGH...  10.1 us
  transfers between devices with their start and end apart: 7, of which 3 were waited for; matrix products, arithmetic and copies ran while one was open for 9% of the time, Pallas kernels for 0%

commit v1 on v0

--- a/solution.py
+++ b/solution.py
@@ -77,7 +77,15 @@
     arrived_all = (
         lax.all_to_all(obs_tiles, ("lat", "lon"), split_axis=1, concat_axis=0, tiled=True),
         lax.all_to_all(tile_block, ("lat", "lon"), split_axis=1, concat_axis=0, tiled=True),
-        lax.all_to_all(tile_rows, ("lat", "lon"), split_axis=1, concat_axis=0, tiled=True),
+        jnp.concatenate(
+            lax.all_to_all(
+                jnp.stack(jnp.split(tile_rows, lax.axis_size(("lat", "lon")), axis=1)),
+                ("lat", "lon"),
+                0,
+                0,
+            ),
+            axis=0,
+        ),
     )
     group_count = block_count // 8
     group_size = 8 * slot_count

time: 270 us -> 345 us (1.28)
  local copies, waits for them, and re-layouts: 53.3 us -> 129 us
    unnamed x28 -> x154, local copies, waits for them, and re-layouts: 2.3 us -> 65.8 us
    split x0 -> x7, local copies, waits for them, and re-layouts: none -> 13 us  [shards(): jnp.split(tile_rows, lax.axis_size(('lat', 'lon')), axis=1)]
  transfers between devices with their start and end apart: 7 -> 7, of which waited for: 3 -> 3; matrix products, arithmetic and copies ran while one was open for 9% -> 7% of each run, Pallas kernels for 0% -> 0%
where the time goes in v1:
time: 345 us; the launch traced here: 344 us
  local copies, waits for them, and re-layouts  129 us (37%)
  waiting for transfers between devices  87.9 us (25%)
  matrix products  69.2 us (20%)
  starting transfers between devices  20.9 us (6%)
  between operations  14.1 us (4%)
  blocking collectives  13.8 us (4%)
  other arithmetic  8.09 us (2%)
    unnamed x154, local copies, waits for them, and re-layouts  65.8 us
    all_gather x1, waiting for transfers between devices, shards(): return lax.all_gather(coarse, 'lon', axis=1, tiled=True)  51.1 us
    dot_general x16, matrix products, tile_terms(): jnp.einsum('tco,tko->tck', features, kernel, preferred_element_type=jnp.f...  42.6 us
    slice x23, local copies, waits for them, and re-layouts, stride_conv(): lax.slice(padded, (row_tap, col_tap, 0), (row_tap + 2 * out_rows - 1, col...  29.4 us
    all_to_all x1, waiting for transfers between devices, shards(): lax.all_to_all(obs_tiles, ('lat', 'lon'), split_axis=1, concat_axis=0, ti...  28 us
    all_to_all x1, blocking collectives, shards(): lax.all_to_all(tile_block, ('lat', 'lon'), split_axis=1, concat_axis=0, t...  13.8 us
    split x7, local copies, waits for them, and re-layouts, shards(): jnp.split(tile_rows, lax.axis_size(('lat', 'lon')), axis=1)  13 us
    dot_general x18, matrix products, stride_conv(): jnp.dot(tap_rows.reshape(-1, padded.shape[2]), weight[3 * row_tap + col_t...  11.6 us
  transfers between devices with their start and end apart: 7, of which 3 were waited for; matrix products, arithmetic and copies ran while one was open for 7% of the time, Pallas kernels for 0%

profile of v1, /device:TPU:1, one launch (start us, length us, event | category | flops | bytes accessed | tf_op | source)
XLA Modules:
  0.0 344.1 jit_solution(15599589830242923165)
XLA Ops:
  85.0 11.5 %all-to-all-start.2 = ((s32[128,1,1,4]{3,2,1,0:T(1,128)}), s32[128,1,1,4]{3,2,1,0:T(1,128)S(1)}, u32[]{:S(2)}, u32[]{:S(2)}) async-start(s32[128,1,1,4]{3,2,1,0:T(1,128)} %constant_dynamic-update-slice_fusion), calls=%async_computation.2 | async-start | bytes 131072 | tf_op jit(solution)/shard_map/all_to_all | solution.py:81
  97.3 8.7 %all-to-all-done.2 = s32[128,1,1,4]{3,2,1,0:T(1,128)S(1)} async-done(((s32[128,1,1,4]{3,2,1,0:T(1,128)}), s32[128,1,1,4]{3,2,1,0:T(1,128)S(1)}, u32[]{:S(2)}, u32[]{:S(2)}) %all-to-all-start.2) | async-done | bytes 2080 | tf_op jit(solution)/shard_map/all_to_all | solution.py:81
  106.1 13.8 %all_to_all.23 = s32[1,128,4]{2,0,1:T(1,128)S(1)} all-to-all(s32[1,128,4]{2,0,1:T(1,128)S(1)} %copy.438), channel_id=1, replica_groups=mesh['lat'=4,'lon'=32] {'lat','lon'}, dimensions={1} | all-to-all | bytes 4096 | tf_op jit(solution)/shard_map/all_to_all | solution.py:79
  119.9 4.4 %all-to-all-start.1 = ((bf16[1,128,4,8,256]{4,3,2,0,1:T(8,128)(2,1)}), bf16[1,128,4,8,256]{4,3,2,0,1:T(8,128)(2,1)S(1)}, u32[]{:S(2)}, u32[]{:S(2)}) async-start(bf16[1,128,4,8,256]{4,3,2,0,1:T(8,128)(2,1)} %bitcast.391), calls=%async_computation.1 | async-start | bytes 4194304 | tf_op jit(solution)/shard_map/all_to_all | solution.py:78
  126.8 28.0 %all-to-all-done.1 = bf16[1,128,4,8,256]{4,3,2,0,1:T(8,128)(2,1)S(1)} async-done(((bf16[1,128,4,8,256]{4,3,2,0,1:T(8,128)(2,1)}), bf16[1,128,4,8,256]{4,3,2,0,1:T(8,128)(2,1)S(1)}, u32[]{:S(2)}, u32[]{:S(2)}) %all-to-all-start.1) | async-done | bytes 2097184 | tf_op jit(solution)/shard_map/all_to_all | solution.py:78
  154.8 61.0 %while.13 = (s32[]{:T(128)}, f32[12,24,256]{2,0,1:T(8,128)S(1)}, s32[16,32]{1,0:T(8,128)S(1)}, bf16[16,32,8,256]{3,2,1,0:T(8,128)(2,1)S(1)}, bf16[6,23]{1,0:T(8,...) while((s32[]{:T(128)}, f32[12,24,256]{2,0,1:T(8,128)S(1)}, ...), condition=%wide.region_1.2_spmd.clone, body=%wide.region_0.1_spmd.clone.sunk | while | flops 150475136 | bytes 3626115 | solution.py:110
  155.3 2.7 fusion.104
  159.1 2.7 fusion.104
  162.9 2.7 fusion.104
  166.7 2.7 fusion.104
  170.5 2.7 fusion.104
  174.4 2.7 fusion.104
  178.2 2.7 fusion.104
  182.0 2.7 fusion.104
  185.8 2.7 fusion.104
  189.6 2.7 fusion.104
  193.4 2.7 fusion.104
  232.7 3.7 %slice.160 = bf16[32,24,24]{0,2,1:T(8,128)(2,1)S(1)} slice(bf16[64,49,24]{0,2,1:T(8,128)(2,1)S(1)} %pad_maximum_fusion.1), slice={[1:64:2], [0:47:2], [0:24:1]} | slice | bytes 73728 | tf_op jit(solution)/shard_map/slice | solution.py:49
  236.4 3.7 %slice.154 = bf16[32,24,24]{0,2,1:T(8,128)(2,1)S(1)} slice(bf16[64,49,24]{0,2,1:T(8,128)(2,1)S(1)} %pad_maximum_fusion.1), slice={[0:63:2], [0:47:2], [0:24:1]} | slice | bytes 73728 | tf_op jit(solution)/shard_map/slice | solution.py:49
  243.3 4.2 %slice.152 = bf16[32,24,24]{0,2,1:T(8,128)(2,1)S(1)} slice(bf16[65,49,24]{0,2,1:T(8,128)(2,1)S(1)} %maximum_maximum_fusion.1), slice={[0:63:2], [2:49:2], [0:24:1]} | slice | bytes 73728 | tf_op jit(solution)/shard_map/slice | solution.py:49
  247.5 3.7 %slice.150 = bf16[32,24,24]{0,2,1:T(8,128)(2,1)S(1)} slice(bf16[65,49,24]{0,2,1:T(8,128)(2,1)S(1)} %maximum_maximum_fusion.1), slice={[0:63:2], [1:48:2], [0:24:1]} | slice | bytes 73728 | tf_op jit(solution)/shard_map/slice | solution.py:49
  251.1 3.7 %slice.148 = bf16[32,24,24]{0,2,1:T(8,128)(2,1)S(1)} slice(bf16[65,49,24]{0,2,1:T(8,128)(2,1)S(1)} %maximum_maximum_fusion.1), slice={[0:63:2], [0:47:2], [0:24:1]} | slice | bytes 73728 | tf_op jit(solution)/shard_map/slice | solution.py:49
  277.1 51.1 %all-gather.2.cloned.1.call-done = bf16[16,384,512]{2,0,1:T(8,128)(2,1)} async-done(((bf16[16,12,512]{2,0,1:T(8,128)(2,1)}), bf16[16,384,512]{2,0,1:T(8,128)(2,1)}) %all-gather.2.cloned.1.call-update) | async-done | bytes 6291472 | tf_op jit(solution)/shard_map/all_gather | solution.py:136
  328.2 9.0 %copy.450 = bf16[16,384,512]{2,1,0:T(8,128)(2,1)} copy(bf16[16,384,512]{2,0,1:T(8,128)(2,1)} %all-gather.2.cloned.1.call-done) | data formatting | bytes 12582912 | tf_op jit(solution)/shard_map/all_gather | solution.py:136
  (382 shorter events, 154.2 us)
Async XLA Ops:
  85.0 21.0 %all-to-all-start.2 = ((s32[128,1,1,4]{3,2,1,0:T(1,128)}), s32[128,1,1,4]{3,2,1,0:T(1,128)S(1)}, u32[]{:S(2)}, u32[]{:S(2)}) async-start(s32[128,1,1,4]{3,2,1,0:T(1,128)} %constant_dynamic-update-slice_fusion), calls=%async_computation.2 | async-start | bytes 131072 | tf_op jit(solution)/shard_map/all_to_all | solution.py:81
  97.3 57.5 %copy-start.10 = (bf16[6,23]{1,0:T(8,128)(2,1)S(1)}, bf16[6,23]{1,0:T(8,128)(2,1)}, u32[]{:S(2)}) copy-start(bf16[6,23]{1,0:T(8,128)(2,1)} %param.13) | copy-start | bytes 832
  119.9 34.9 %all-to-all-start.1 = ((bf16[1,128,4,8,256]{4,3,2,0,1:T(8,128)(2,1)}), bf16[1,128,4,8,256]{4,3,2,0,1:T(8,128)(2,1)S(1)}, u32[]{:S(2)}, u32[]{:S(2)}) async-start(bf16[1,128,4,8,256]{4,3,2,0,1:T(8,128)(2,1)} %bitcast.391), calls=%async_computation.1 | async-start | bytes 4194304 | tf_op jit(solution)/shard_map/all_to_all | solution.py:78
  124.3 203.9 %all-gather.2.cloned.1.call-start = ((), (), s32[]{:S(2)}) async-start(), calls=%async_computation.3 | async-start | bytes 6488064 | tf_op jit(solution)/shard_map/all_gather | solution.py:136
  223.3 6.4 %collective-permute-start = (bf16[64,1,24]{2,1,0:T(2,128)(2,1)S(1)}, bf16[64,1,24]{2,1,0:T(2,128)(2,1)S(1)}, u32[]{:S(2)}, u32[]{:S(2)}) collective-permute-start(bf16[64,1,24]{2,1,0:T(2,128)(2,1)S(1)} %slice.192), channel_id=1, source_target_pairs={{0,1},{1,2},{2,3},{3,4},{4,5},{5,6},{6,7},{7,8},{8,9},{9,10},{10,1... | collective-permute-start | bytes 9224 | tf_op jit(solution)/shard_map/ppermute | solution.py:14
  230.6 11.5 %collective-permute-start.1 = (bf16[1,49,24]{0,2,1:T(8,128)(2,1)}, bf16[1,49,24]{0,2,1:T(8,128)(2,1)}, u32[]{:S(2)}, u32[]{:S(2)}) collective-permute-start(bf16[1,49,24]{0,2,1:T(8,128)(2,1)} %fusion.25), channel_id=1, source_target_pairs={{0,32},{32,64},{64,96},{1,33},{33,65},{65,97},{2,34},{34,66},{66,9... | collective-permute-start | bytes 7064 | tf_op jit(solution)/shard_map/ppermute | solution.py:20
  256.3 3.5 %copy-start = (f32[768,256]{1,0:T(8,128)S(1)}, f32[768,256]{1,0:T(8,128)}, u32[]{:S(2)}) copy-start(f32[768,256]{1,0:T(8,128)} %fusion.51) | copy-start | bytes 2359300
  256.4 3.4 copy-start.9
  258.8 2.1 copy-start.8
  260.8 1.0 copy-start.12
  262.1 5.1 %collective-permute-start.2 = (bf16[32,1,256]{2,1,0:T(2,128)(2,1)S(1)}, bf16[32,1,256]{2,1,0:T(2,128)(2,1)S(1)}, u32[]{:S(2)}, u32[]{:S(2)}) collective-permute-start(bf16[32,1,256]{2,1,0:T(2,128)(2,1)S(1)} %slice.195), channel_id=1, source_target_pairs={{0,1},{1,2},{2,3},{3,4},{4,5},{5,6},{6,7},{7,8},{8,9},{9,10},{10,1... | collective-permute-start | bytes 49160 | tf_op jit(solution)/shard_map/ppermute | solution.py:14
  267.2 6.9 %copy-start.1 = (bf16[9,256,512]{2,1,0:T(8,128)(2,1)S(1)}, bf16[9,256,512]{2,1,0:T(8,128)(2,1)}, u32[]{:S(2)}) copy-start(bf16[9,256,512]{2,1,0:T(8,128)(2,1)} %param.16) | copy-start | bytes 7077892
  267.2 2.5 copy-start.7
  267.8 3.9 %collective-permute-start.3 = (bf16[1,25,256]{2,1,0:T(8,128)(2,1)}, bf16[1,25,256]{2,1,0:T(8,128)(2,1)S(1)}, u32[]{:S(2)}, u32[]{:S(2)}) collective-permute-start(bf16[1,25,256]{2,1,0:T(8,128)(2,1)} %fusion.45), channel_id=1, source_target_pairs={{0,32},{32,64},{64,96},{1,33},{33,65},{65,97},{2,34},{34,66},{66,9... | collective-permute-start | bytes 38408 | tf_op jit(solution)/shard_map/ppermute | solution.py:20
  272.7 2.0 copy-start.6
  274.0 1.0 copy-start.5
  274.3 0.9 copy-start.4
  274.8 0.9 copy-start.3
  275.0 0.9 copy-start.2
  275.4 0.7 copy-start.11
Sparse Core Ops, SparseCore 0:
  277.2 50.9 all-gather.1
